TPU v7x, 32 devices: a whole 2x2x4 slice. The times are simulated.
32 devices in a mesh: grp: 2 (over x), col: 16 (over z, y, core).
Axes of the slice: x: 2, y: 2, z: 4, core: 2. Of those that a mesh axis runs over, the one named last changes fastest.
Arguments:
- lam_in: float32 [320, 4, 32, 128], P('grp', None, 'col'), parts along dimension 0, may hold values from -0.5 to 1.5
- conc: float32 [320, 4, 32, 128], P('grp', None, 'col'), parts along dimension 0, may hold values from 0.3 to 3
- jac_diag: bfloat16 [20, 16, 16, 4, 32, 128], P('grp', None, None, None, 'col'), parts along dimension 0, may hold values from -0.59765625 to 0.59765625
- jac_off: bfloat16 [8, 16, 16, 4, 32, 128], P('grp', None, None, None, 'col'), parts along dimension 0, may hold values from -0.59765625 to 0.59765625
- block_rows: int32 [8, 4, 32, 128], P('grp', None, 'col'), parts along dimension 0, may hold values from 0 to 9
- block_cols: int32 [8, 4, 32, 128], P('grp', None, 'col'), parts along dimension 0, may hold values from 0 to 9
- active: int32 [8, 32, 128], P('grp', 'col'), parts along dimension 0, may hold values from 0 to 4
- courant: float32 [2, 8, 32, 128], P(None, 'grp', 'col'), parts along dimension 1, may hold values from 0.05 to 0.45
- kz: float32 [6, 32, 128], P('grp', 'col'), parts along dimension 0, may hold values from 0.1 to 3
- airmass: float32 [8, 32, 128], P('grp', 'col'), parts along dimension 0, may hold values from 0.5 to 6, as said below
- target: float32 [320], P('grp'), parts along dimension 0, may hold values from 0.5 to 2
- emis_map: float32 [64, 160], replicated, may hold values from -0.5 to 0.5
Outputs:
- lam_out: float32 [320, 4, 32, 128], P('grp', None, 'col'), parts along dimension 0
- grad_emis: float32 [128, 32, 128], P('grp', 'col'), parts along dimension 0
There are 2 independent parts, one for each index of `grp`. A program takes and returns all parts, laid end to end along the dimension named above; an argument that names none is the same for every part. Nothing has to cross between parts.
Inputs may be any that keep to these rules, and one draw needn't show every extreme that they name: airmass is positive. Slots p >= active[cell] are ignored.
All inputs are finite; a program needn't handle non-finite values.
Results may differ from a plain program's by a relative error of at most 0.0003.
Values sent between devices are 32-bit elements; how exact they have to be, the bound alone decides.
A program may use at most 64 MiB of HBM per device.

v0:
```python
import jax
import jax.numpy as jnp
from jax import lax
from jax.sharding import PartitionSpec as P

ADV = 2


def with_halo(cells, sides, width):
    for axis, dim in sides:
        count = lax.axis_size(axis)
        ends = count - 1
        head = lax.slice_in_dim(cells, 0, width, axis=dim)
        tail = lax.slice_in_dim(cells, cells.shape[dim] - width, cells.shape[dim], axis=dim)
        cells = jnp.concatenate(
            [
                lax.ppermute(tail, axis, [(i, (i + 1) % count) for i in range(ends)]),
                cells,
                lax.ppermute(head, axis, [((i + 1) % count, i) for i in range(ends)]),
            ],
            axis=dim,
        )
    return cells


def chem_adjoint(lam, jac_diag, jac_off, block_rows, block_cols, active):
    nblocks = jac_diag.shape[0]
    bsize = jac_diag.shape[1]
    lamb = lam.reshape((nblocks, bsize) + lam.shape[1:])
    result = lamb + jnp.einsum(
        "bij...,bi...->bj...", jac_diag.astype(jnp.float32), lamb, precision=lax.Precision.HIGHEST
    )
    blocks = jnp.arange(nblocks, dtype=jnp.int32)
    for slot in range(jac_off.shape[0]):
        pick = (block_rows[slot][None] == blocks[:, None, None, None]).astype(jnp.float32)
        chosen = jnp.sum(pick[:, None] * lamb, axis=0)
        live = (active > slot).astype(jnp.float32)
        contrib = (
            jnp.einsum(
                "ij...,i...->j...",
                jac_off[slot].astype(jnp.float32),
                chosen,
                precision=lax.Precision.HIGHEST,
            )
            * live[None]
        )
        place = (block_cols[slot][None] == blocks[:, None, None, None]).astype(jnp.float32)
        result = result + place[:, None] * contrib[None]
    return result.reshape(lam.shape)


def solve_levels(kz, rhs):
    levels = rhs.shape[1]
    diag = []
    for lev in range(levels):
        value = jnp.ones_like(rhs[0, 0])
        if lev > 0:
            value = value + kz[lev - 1]
        if lev < levels - 1:
            value = value + kz[lev]
        diag.append(value)
    cprime = []
    dprime = []
    for lev in range(levels):
        denom = diag[lev]
        numer = rhs[:, lev]
        if lev > 0:
            denom = denom + kz[lev - 1] * cprime[lev - 1]
            numer = numer + kz[lev - 1] * dprime[lev - 1]
        denom = denom[None]
        cval = -kz[lev][None] / denom if lev < levels - 1 else None
        cprime.append(cval[0] if cval is not None else None)
        dprime.append(numer / denom)
    solved = [None] * levels
    solved[levels - 1] = dprime[levels - 1]
    for lev in range(levels - 2, -1, -1):
        solved[lev] = dprime[lev] - cprime[lev][None] * solved[lev + 1]
    return jnp.stack(solved, axis=1)


def apply_step(padded, right_out, left_out):
    return (
        padded[:, :, 1:-1] * (1.0 - right_out - left_out)
        + left_out * padded[:, :, :-2]
        + right_out * padded[:, :, 2:]
    )


def body(
    lam_in,
    conc,
    jac_diag,
    jac_off,
    block_rows,
    block_cols,
    active,
    courant,
    kz,
    airmass,
    target,
    emis_map,
):
    cells = lam_in.shape[1] * lam_in.shape[2] * lam_in.shape[3] * lax.axis_size("col")
    mass_local = jnp.sum(conc * airmass[None], axis=(1, 2, 3))
    lam = chem_adjoint(lam_in, jac_diag, jac_off, block_rows, block_cols, active)
    quad_local = jnp.sum(conc * lam, axis=(1, 2, 3))
    mass, quad = lax.psum((mass_local, quad_local), "col")
    scale = target * cells / mass
    lam = (
        lam * scale[:, None, None, None]
        - airmass[None] * (scale * quad / mass)[:, None, None, None]
    )
    lam = solve_levels(kz, lam)
    for step in range(ADV):
        padded = with_halo(lam, (("col", 2),), 1)
        lam = apply_step(padded, courant[0][None], courant[1][None])
    grad_emis = jnp.einsum("es,sxy->exy", emis_map, lam[:, 0], precision=lax.Precision.HIGHEST)
    return (lam, grad_emis)


def solution(mesh):
    return jax.shard_map(
        body,
        mesh=mesh,
        in_specs=(
            P("grp", None, "col", None),
            P("grp", None, "col", None),
            P("grp", None, None, None, "col", None),
            P("grp", None, None, None, "col", None),
            P("grp", None, "col", None),
            P("grp", None, "col", None),
            P("grp", "col", None),
            P(None, "grp", "col", None),
            P("grp", "col", None),
            P("grp", "col", None),
            P("grp"),
            P(),
        ),
        out_specs=(P("grp", None, "col", None), P("grp", "col", None)),
        check_vma=False,
    )
```

profile of v0, /device:TPU:4, one launch (start us, length us, event | category | flops | bytes accessed | tf_op | source)
XLA Modules:
  0.0 76.4 jit_solution(4952871277366676331)
XLA Ops:
  0.6 0.0 copy-start
  0.6 0.0 copy-start.1
  0.7 0.8 %slice_bitcast_fusion.2 = (s32[4,2,128]{2,1,0:T(2,128)S(1)}, s32[4,2,128]{2,1,0:T(2,128)S(1)}, s32[4,2,128]{2,1,0:T(2,128)S(1)}, s32[4,2,128]{2,1,0:T(2,128)S(1)}) fusion(s32[4,4,2,128]{3,2,1,0:T(2,128)} %param.16), kind=kLoop, calls=%fused_computation.74 | loop fusion | bytes 32768 | tf_op jit(solution)/shard_map/eq | solution.py:35
  1.5 0.7 compare_convert_fusion.7
  2.2 0.7 slice_bitcast_fusion.9
  2.9 0.7 slice_bitcast_fusion.14
  3.7 2.3 %multiply_reduce_fusion.10 = (f32[16,4,2,128]{3,2,1,0:T(2,128)S(1)}, f32[16,4,2,128]{3,2,1,0:T(2,128)S(1)}, f32[16,4,2,128]{3,2,1,0:T(2,128)S(1)}, f32[16,4,2,128]{3,2,1,0:T(2,128)S(1)}) fusion(f32[10,16,4,2,128]{4,3,2,1,0:T(2,128)} %bitcast.91, f32[10,4,2,128]{3,2,1,0:T(2,128)S(1)} %get-tuple-element.59, f32[10,4,2,128]{3,2,1,0:T(2,128)S(1)} %get-tuple-element.57, ...), kind=kLoop, calls=%fused_computation.36 | loop fusion | flops 1245184 | bytes 1081344 | tf_op jit(solution)/shard_map/reduce_sum | solution.py:36
  6.1 3.8 %multiply_reduce_fusion.4 = (f32[4,2,128,16]{2,1,0,3:T(2,128)S(1)}, f32[4,2,128,16]{2,1,0,3:T(2,128)S(1)}, f32[4,2,128,16]{2,1,0,3:T(2,128)S(1)}, f32[4,2,128,16]{2,1,0,3:T(2,128)S(1)}) fusion(f32[4,2,128,16]{2,1,0,3:T(2,128)S(1)} %bitcast.95, bf16[4,16,16,4,2,128]{5,4,3,2,1,0:T(2,128)(2,1)} %param.15, f32[4,2,128,16]{2,1,0,3:T(2,128)S(1)} %bitcast.97, ...), kind=kLoop, calls=%fused_computation.5 | loop fusion | flops 3080192 | bytes 2621440
  9.9 0.0 copy-start.2
  9.9 0.0 copy-start.3
  10.0 0.0 copy-start.5
  10.0 0.0 copy-done.1
  10.0 9.7 %multiply_reduce_fusion = f32[10,4,2,128,16]{3,2,1,4,0:T(2,128)S(1)} fusion(f32[10,4,2,128,16]{3,2,1,4,0:T(2,128)S(1)} %bitcast.92, bf16[10,16,16,4,2,128]{5,4,3,2,1,0:T(2,128)(2,1)} %param.14), kind=kLoop, calls=%fused_computation | loop fusion | flops 7700480 | bytes 6553600
  19.8 0.0 copy-start.4
  19.8 0.4 fusion.11
  20.2 0.3 multiply_reduce_fusion.5
  20.5 29.0 %all-reduce = (f32[160]{0:T(256)S(1)}, f32[160]{0:T(256)S(1)}) all-reduce(f32[160]{0:T(256)S(1)} %get-tuple-element.9, f32[160]{0:T(256)S(1)} %get-tuple-element.8), channel_id=1, replica_groups=mesh['grp'=2,'col'=16] {'col'}, use_global_device_ids=true, to_apply=%region_5.0 | all-reduce | flops 320 | bytes 2560 | tf_op jit(solution)/shard_map/psum | solution.py:107
  49.6 0.2 multiply_subtract_fusion
  49.7 0.1 multiply_subtract_fusion.1
  50.0 1.9 %collective-permute-start = (f32[160,4,1,128]{3,0,2,1:T(8,128)S(1)}, f32[160,4,1,128]{3,0,2,1:T(8,128)S(1)}, u32[]{:S(2)}, u32[]{:S(2)}) collective-permute-start(f32[160,4,1,128]{3,0,2,1:T(8,128)S(1)} %get-tuple-element.29), channel_id=1, source_target_pairs={{0,1},{1,2},{2,3},{3,4},{4,5},{5,6},{6,7},{7,8},{8,9},{9,10},{10,1... | collective-permute-start | bytes 983048 | tf_op jit(solution)/shard_map/ppermute | solution.py:17
  51.9 3.6 %collective-permute-start.1 = (f32[160,4,1,128]{3,0,2,1:T(8,128)S(1)}, f32[160,4,1,128]{3,0,2,1:T(8,128)S(1)}, u32[]{:S(2)}, u32[]{:S(2)}) collective-permute-start(f32[160,4,1,128]{3,0,2,1:T(8,128)S(1)} %get-tuple-element.30), channel_id=1, source_target_pairs={{1,0},{2,1},{3,2},{4,3},{5,4},{6,5},{7,6},{8,7},{9,8},{10,9},{11,1... | collective-permute-start | bytes 983048 | tf_op jit(solution)/shard_map/ppermute | solution.py:19
  55.6 6.3 %collective-permute-done = f32[160,4,1,128]{3,0,2,1:T(8,128)S(1)} collective-permute-done((f32[160,4,1,128]{3,0,2,1:T(8,128)S(1)}, f32[160,4,1,128]{3,0,2,1:T(8,128)S(1)}, u32[]{:S(2)}, u32[]{:S(2)}) %collective-permute-start) | collective-permute-done | bytes 327712 | tf_op jit(solution)/shard_map/ppermute | solution.py:17
  61.9 0.0 collective-permute-done.1
  61.9 0.1 fusion.5
  62.1 1.9 %collective-permute-start.2 = (f32[160,4,1,128]{3,0,2,1:T(8,128)S(1)}, f32[160,4,1,128]{3,0,2,1:T(8,128)S(1)}, u32[]{:S(2)}, u32[]{:S(2)}) collective-permute-start(f32[160,4,1,128]{3,0,2,1:T(8,128)S(1)} %get-tuple-element.27), channel_id=1, source_target_pairs={{0,1},{1,2},{2,3},{3,4},{4,5},{5,6},{6,7},{7,8},{8,9},{9,10},{10,1... | collective-permute-start | bytes 983048 | tf_op jit(solution)/shard_map/ppermute | solution.py:17
  64.0 3.6 %collective-permute-start.3 = (f32[160,4,1,128]{3,0,2,1:T(8,128)S(1)}, f32[160,4,1,128]{3,0,2,1:T(8,128)S(1)}, u32[]{:S(2)}, u32[]{:S(2)}) collective-permute-start(f32[160,4,1,128]{3,0,2,1:T(8,128)S(1)} %get-tuple-element.28), channel_id=1, source_target_pairs={{1,0},{2,1},{3,2},{4,3},{5,4},{6,5},{7,6},{8,7},{9,8},{10,9},{11,1... | collective-permute-start | bytes 983048 | tf_op jit(solution)/shard_map/ppermute | solution.py:19
  67.6 6.3 %collective-permute-done.2 = f32[160,4,1,128]{3,0,2,1:T(8,128)S(1)} collective-permute-done((f32[160,4,1,128]{3,0,2,1:T(8,128)S(1)}, f32[160,4,1,128]{3,0,2,1:T(8,128)S(1)}, u32[]{:S(2)}, u32[]{:S(2)}) %collective-permute-start.2) | collective-permute-done | bytes 327712 | tf_op jit(solution)/shard_map/ppermute | solution.py:17
  74.0 0.0 collective-permute-done.3
  74.0 0.1 fusion.1
  74.1 1.3 %copy.17 = f32[160,4,2,128]{3,2,1,0:T(2,128)} copy(f32[160,4,2,128]{3,0,2,1:T(8,128)S(1)} %fusion.1) | data formatting | bytes 1310720
  75.4 0.2 convolution_bitcast_fusion
  75.7 0.7 copy.18
  (19 shorter events, 0.4 us)
Async XLA Ops:
  0.6 74.8 %copy-start = (f32[64,160]{1,0:T(8,128)S(1)}, f32[64,160]{1,0:T(8,128)}, u32[]{:S(2)}) copy-start(f32[64,160]{1,0:T(8,128)} %param.23) | copy-start | bytes 122884
  0.6 9.4 %copy-start.1 = (f32[160,4,2,128]{3,2,1,0:T(2,128)S(1)}, f32[160,4,2,128]{3,2,1,0:T(2,128)}, u32[]{:S(2)}) copy-start(f32[160,4,2,128]{3,2,1,0:T(2,128)} %param.12) | copy-start | bytes 1966084
  9.9 10.4 %copy-start.2 = (f32[160,4,2,128]{3,2,1,0:T(2,128)S(1)}, f32[160,4,2,128]{3,2,1,0:T(2,128)}, u32[]{:S(2)}) copy-start(f32[160,4,2,128]{3,2,1,0:T(2,128)} %param.13) | copy-start | bytes 1966084
  9.9 10.4 %copy-start.3 = (f32[4,2,128]{2,1,0:T(2,128)S(1)}, f32[4,2,128]{2,1,0:T(2,128)}, u32[]{:S(2)}) copy-start(f32[4,2,128]{2,1,0:T(2,128)} %param.21) | copy-start | bytes 12292
  10.0 39.6 %copy-start.5 = (f32[160]{0:T(256)S(1)}, f32[160]{0:T(256)}, u32[]{:S(2)}) copy-start(f32[160]{0:T(256)} %param.22) | copy-start | bytes 1924
  19.8 35.8 %copy-start.4 = (f32[2,4,2,128]{3,2,1,0:T(2,128)S(1)}, f32[2,4,2,128]{3,2,1,0:T(2,128)}, u32[]{:S(2)}) copy-start(f32[2,4,2,128]{3,2,1,0:T(2,128)} %param.19) | copy-start | bytes 24580
  50.0 11.9 %collective-permute-start = (f32[160,4,1,128]{3,0,2,1:T(8,128)S(1)}, f32[160,4,1,128]{3,0,2,1:T(8,128)S(1)}, u32[]{:S(2)}, u32[]{:S(2)}) collective-permute-start(f32[160,4,1,128]{3,0,2,1:T(8,128)S(1)} %get-tuple-element.29), channel_id=1, source_target_pairs={{0,1},{1,2},{2,3},{3,4},{4,5},{5,6},{6,7},{7,8},{8,9},{9,10},{10,1... | collective-permute-start | bytes 983048 | tf_op jit(solution)/shard_map/ppermute | solution.py:17
  51.9 10.0 %collective-permute-start.1 = (f32[160,4,1,128]{3,0,2,1:T(8,128)S(1)}, f32[160,4,1,128]{3,0,2,1:T(8,128)S(1)}, u32[]{:S(2)}, u32[]{:S(2)}) collective-permute-start(f32[160,4,1,128]{3,0,2,1:T(8,128)S(1)} %get-tuple-element.30), channel_id=1, source_target_pairs={{1,0},{2,1},{3,2},{4,3},{5,4},{6,5},{7,6},{8,7},{9,8},{10,9},{11,1... | collective-permute-start | bytes 983048 | tf_op jit(solution)/shard_map/ppermute | solution.py:19
  62.1 11.9 %collective-permute-start.2 = (f32[160,4,1,128]{3,0,2,1:T(8,128)S(1)}, f32[160,4,1,128]{3,0,2,1:T(8,128)S(1)}, u32[]{:S(2)}, u32[]{:S(2)}) collective-permute-start(f32[160,4,1,128]{3,0,2,1:T(8,128)S(1)} %get-tuple-element.27), channel_id=1, source_target_pairs={{0,1},{1,2},{2,3},{3,4},{4,5},{5,6},{6,7},{7,8},{8,9},{9,10},{10,1... | collective-permute-start | bytes 983048 | tf_op jit(solution)/shard_map/ppermute | solution.py:17
  64.0 10.0 %collective-permute-start.3 = (f32[160,4,1,128]{3,0,2,1:T(8,128)S(1)}, f32[160,4,1,128]{3,0,2,1:T(8,128)S(1)}, u32[]{:S(2)}, u32[]{:S(2)}) collective-permute-start(f32[160,4,1,128]{3,0,2,1:T(8,128)S(1)} %get-tuple-element.28), channel_id=1, source_target_pairs={{1,0},{2,1},{3,2},{4,3},{5,4},{6,5},{7,6},{8,7},{9,8},{10,9},{11,1... | collective-permute-start | bytes 983048 | tf_op jit(solution)/shard_map/ppermute | solution.py:19
where the time goes:
time: 77.8 us; the launch traced here: 76.4 us
  blocking collectives  29 us (37%)
  other arithmetic  18.8 us (24%)
  waiting for transfers between devices  12.6 us (16%)
  starting transfers between devices  11.1 us (14%)
  local copies, waits for them, and re-layouts  3.7 us (5%)
  between operations  0.89 us (1%)
    psum x1, blocking collectives, body(): mass, quad = lax.psum((mass_local, quad_local), 'col')  29 us
    unnamed x2, other arithmetic  13.5 us
    ppermute x2, waiting for transfers between devices, with_halo(): lax.ppermute(tail, axis, [(i, (i + 1) % count) for i in range(ends)])  12.6 us
    ppermute x2, starting transfers between devices, with_halo(): lax.ppermute(head, axis, [((i + 1) % count, i) for i in range(ends)])  7.28 us
    ppermute x2, starting transfers between devices, with_halo(): lax.ppermute(tail, axis, [(i, (i + 1) % count) for i in range(ends)])  3.84 us
    reduce_sum x1, other arithmetic, chem_adjoint(): chosen = jnp.sum(pick[:, None] * lamb, axis=0)  2.35 us
    unnamed x14, local copies, waits for them, and re-layouts  2.07 us
  transfers between devices with their start and end apart: 4, of which 2 were waited for; matrix products, arithmetic and copies ran while one was open for 0% of the time, Pallas kernels for 0%

commit v1 on v0

v1 whole, which is shorter than its diff:
```python
import functools

import jax
import jax.numpy as jnp
from jax import lax
from jax.experimental import pallas as pl
from jax.experimental.pallas import tpu as pltpu
from jax.sharding import PartitionSpec as P

ADV = 2
ROWS = 8
LANES = 128
F32 = jnp.float32


def inverse_levels(kz):
    levels = len(kz) + 1
    diag = []
    for lev in range(levels):
        value = jnp.ones_like(kz[0])
        if lev > 0:
            value = value + kz[lev - 1]
        if lev < levels - 1:
            value = value + kz[lev]
        diag.append(value)
    cprime, recip = [], []
    for lev in range(levels):
        denom = diag[lev]
        if lev > 0:
            denom = denom + kz[lev - 1] * cprime[lev - 1]
        recip.append(1.0 / denom)
        cprime.append(-kz[lev] * recip[lev] if lev < levels - 1 else None)
    result = [[None] * levels for _ in range(levels)]
    for unit in range(levels):
        dprime = []
        for lev in range(levels):
            if lev < unit:
                dprime.append(jnp.zeros_like(kz[0]))
            elif lev == unit:
                dprime.append(recip[lev])
            else:
                dprime.append(kz[lev - 1] * dprime[lev - 1] * recip[lev])
        solved = dprime[levels - 1]
        result[levels - 1][unit] = solved
        for lev in range(levels - 2, -1, -1):
            solved = dprime[lev] - cprime[lev] * solved
            result[lev][unit] = solved
    return result


def up(x):
    return pltpu.roll(x, ROWS - 1, x.ndim - 2)


def down(x):
    return pltpu.roll(x, 1, x.ndim - 2)


def kernel(
    nblocks, bsize, slots, levels, cells, n,
    lam_h, conc_h, jd_h, jo_h, rows_h, cols_h, act_h, cour_h, kz_h, air_h, target_h, emis_h,
    out_h, grad_h,
    lam, conc, jd, jo, rows, cols, act, cour, kz, air, target, emis,
    l0, left, right, out, grad, contrib, solve, small, small_l, small_r,
    part, stat, stats, scol, gcol,
    in_sem, jo_sem, jd_sem, out_sem, send_r, send_l, recv_l, recv_r, ssem, stat_send, stat_recv,
):
    me = lax.axis_index("col")
    species = nblocks * bsize
    bl = bsize * ROWS
    step = bsize * bl

    def peer(k):
        return lax.rem(me + k, n)

    barrier = pltpu.get_barrier_semaphore()

    @pl.loop(1, n)
    def _(k):
        pl.semaphore_signal(
            barrier, inc=1, device_id={"col": peer(k)}, device_id_type=pl.DeviceIdType.MESH
        )

    plain = [
        pltpu.make_async_copy(src, dst, in_sem.at[k])
        for k, (src, dst) in enumerate(
            [
                (lam_h, lam), (rows_h, rows), (cols_h, cols), (act_h, act), (kz_h, kz),
                (cour_h, cour), (air_h, air), (target_h, target), (emis_h, emis), (conc_h, conc),
            ]
        )
    ]

    def jo_copy(p):
        at = pl.ds(pl.multiple_of(p * step, step), step)
        return pltpu.make_async_copy(jo_h.at[at], jo.at[at], jo_sem.at[p])

    def jd_copy(c):
        at = pl.ds(pl.multiple_of(c * step, step), step)
        return pltpu.make_async_copy(jd_h.at[at], jd.at[at], jd_sem.at[c])

    for copy in plain[:8]:
        copy.start()
    for p in range(slots):
        jo_copy(p).start()
    for c in range(nblocks):
        jd_copy(c).start()
        if c == 0:
            plain[9].start()
    plain[8].start()

    @pl.when(me == 0)
    def _():
        left[...] = jnp.zeros_like(left)
        small_l[...] = jnp.zeros_like(small_l)

    @pl.when(me == n - 1)
    def _():
        right[...] = jnp.zeros_like(right)
        small_r[...] = jnp.zeros_like(small_r)

    for copy in plain[1:8]:
        copy.wait()

    kzs = [kz[lev] for lev in range(levels - 1)]
    inverse = inverse_levels(kzs)
    for shift in range(levels):
        for lev in range(levels):
            solve[shift, 2 * lev : 2 * lev + 2, :] = inverse[lev][(lev - shift) % levels]

    def solve_levels(x):
        total = x * solve[0]
        for shift in range(1, levels):
            total = total + pltpu.roll(x, 2 * shift, x.ndim - 2) * solve[shift]
        return total

    small[0:8, :] = cour[0:8, :]
    small[8:16, :] = cour[8:16, :]
    small[16:24, :] = solve_levels(air[...])

    plain[0].wait()

    @pl.loop(0, slots)
    def _(p):
        live = act[...] > p
        want = jnp.where(live, rows[pl.ds(pl.multiple_of(p * ROWS, ROWS), ROWS), :], -1)
        chosen = jnp.zeros((bsize, ROWS, LANES), F32)
        for b in range(nblocks):
            block = lam[b * bl : (b + 1) * bl, :].reshape(bsize, ROWS, LANES)
            chosen = jnp.where((want == b)[None], block, chosen)
        jo_copy(p).wait()
        acc = jnp.zeros((bsize, ROWS, LANES), F32)
        for i in range(bsize):
            at = pl.ds(pl.multiple_of(p * step + i * bl, bl), bl)
            acc = acc + jo[at, :].astype(F32).reshape(bsize, ROWS, LANES) * chosen[i][None]
        contrib[p] = acc

    pl.semaphore_wait(barrier, n - 1)

    def to_right(src, dst, ssem_, rsem):
        return pltpu.make_async_remote_copy(
            src_ref=src, dst_ref=dst, send_sem=ssem_, recv_sem=rsem,
            device_id={"col": jnp.minimum(me + 1, n - 1)}, device_id_type=pl.DeviceIdType.MESH,
        )

    def to_left(src, dst, ssem_, rsem):
        return pltpu.make_async_remote_copy(
            src_ref=src, dst_ref=dst, send_sem=ssem_, recv_sem=rsem,
            device_id={"col": jnp.maximum(me - 1, 0)}, device_id_type=pl.DeviceIdType.MESH,
        )

    def block_at(c):
        return pl.ds(pl.multiple_of(c * bl, bl), bl)

    def block_right(c):
        return to_right(l0.at[block_at(c)], left.at[block_at(c)], send_r.at[c], recv_l.at[c])

    def block_left(c):
        return to_left(l0.at[block_at(c)], right.at[block_at(c)], send_l.at[c], recv_r.at[c])

    small_right = to_right(small, small_l, ssem.at[0], ssem.at[1])
    small_left = to_left(small, small_r, ssem.at[2], ssem.at[3])

    @pl.when(me < n - 1)
    def _():
        small_right.start()

    @pl.when(me > 0)
    def _():
        small_left.start()

    plain[9].wait()

    @pl.loop(0, nblocks)
    def _(c):
        block = lam[block_at(c), :].reshape(bsize, ROWS, LANES)
        jd_copy(c).wait()
        acc = block
        for i in range(bsize):
            at = pl.ds(pl.multiple_of(c * step + i * bl, bl), bl)
            acc = acc + jd[at, :].astype(F32).reshape(bsize, ROWS, LANES) * block[i][None]
        for p in range(slots):
            place = cols[p * ROWS : (p + 1) * ROWS, :] == c
            acc = acc + jnp.where(place[None], contrib[p], 0.0)
        l0[block_at(c), :] = solve_levels(acc).reshape(bl, LANES)

        @pl.when(me < n - 1)
        def _():
            block_right(c).start()

        @pl.when(me > 0)
        def _():
            block_left(c).start()

        amount = conc[block_at(c), :].reshape(bsize, ROWS, LANES)
        at = pl.ds(pl.multiple_of(c * bsize, bsize), bsize)
        part[0, at, :] = jnp.sum(amount * air[...][None], axis=1)
        part[1, at, :] = jnp.sum(amount * acc, axis=1)

    tail = species - LANES
    for which in range(2):
        for half, first in enumerate((0, tail)):
            square = part[which, first : first + LANES, :]
            stat[2 * which + half : 2 * which + half + 1, :] = jnp.sum(
                square.T, axis=0, keepdims=True
            )

    def stat_copy(k):
        return pltpu.make_async_remote_copy(
            src_ref=stat, dst_ref=stats.at[me], send_sem=stat_send.at[k], recv_sem=stat_recv.at[me],
            device_id={"col": peer(k)}, device_id_type=pl.DeviceIdType.MESH,
        )

    def stat_from(k):
        source = lax.rem(me + n - k, n)
        return source, pltpu.make_async_remote_copy(
            src_ref=stat, dst_ref=stats.at[source], send_sem=stat_send.at[k],
            recv_sem=stat_recv.at[source],
            device_id={"col": peer(k)}, device_id_type=pl.DeviceIdType.MESH,
        )

    @pl.loop(1, n)
    def _(k):
        stat_copy(k).start()

    @pl.when(me > 0)
    def _():
        to_right(small, small_l, ssem.at[0], ssem.at[1]).wait_recv()

    @pl.when(me < n - 1)
    def _():
        to_left(small, small_r, ssem.at[2], ssem.at[3]).wait_recv()

    even = lax.rem(lax.broadcasted_iota(jnp.int32, (ROWS, LANES), 0), 2) == 0

    def swap(x):
        return jnp.where(even, up(x), down(x))

    a, b = small[0:8, :], small[8:16, :]
    c = 1.0 - a - b
    al, bl_ = small_l[0:8, :], small_l[8:16, :]
    cl = 1.0 - al - bl_
    ar, br = small_r[0:8, :], small_r[8:16, :]
    cr = 1.0 - ar - br
    own_same = c * c + jnp.where(even, b * swap(al) + a * swap(b), b * swap(a) + a * swap(br))
    own_swap = jnp.where(even, a, b) * (c + swap(c))
    left_same = b * jnp.where(even, swap(bl_), swap(b))
    left_up = jnp.where(even, b * (c + swap(cl)), 0.0)
    right_same = a * jnp.where(even, swap(a), swap(ar))
    right_down = jnp.where(even, 0.0, a * (c + swap(cr)))

    def advect(mid, lt, rt):
        return (
            own_same * mid
            + own_swap * jnp.where(even, up(mid), down(mid))
            + left_same * lt
            + left_up * up(lt)
            + right_same * rt
            + right_down * down(rt)
        )

    air_out = advect(small[16:24, :], small_l[16:24, :], small_r[16:24, :])

    def add_stat(k, total):
        source, copy = stat_from(k)
        copy.wait_recv()
        return total + stats[source]

    total = lax.fori_loop(1, n, add_stat, stat[...])
    for half, first in enumerate((0, tail)):
        mass = total[half : half + 1, :]
        quad = total[2 + half : 3 + half, :]
        scale = target[:, first : first + LANES] * float(cells) / mass
        gain = scale * quad / mass
        scol[first : first + LANES, :] = jnp.broadcast_to(scale, (LANES, LANES)).T
        gcol[first : first + LANES, :] = jnp.broadcast_to(gain, (LANES, LANES)).T

    def out_copy(c):
        return pltpu.make_async_copy(out.at[block_at(c)], out_h.at[block_at(c)], out_sem.at[c])

    @pl.loop(0, nblocks)
    def _(c):
        @pl.when(me > 0)
        def _():
            block_right(c).wait_recv()

        @pl.when(me < n - 1)
        def _():
            block_left(c).wait_recv()

        at = block_at(c)
        shape = (bsize, ROWS, LANES)
        moved = advect(l0[at, :].reshape(shape), left[at, :].reshape(shape), right[at, :].reshape(shape))
        names = pl.ds(pl.multiple_of(c * bsize, bsize), bsize)
        result = scol[names, :][:, None, :] * moved - gcol[names, :][:, None, :] * air_out[None]
        out[at, :] = result.reshape(bl, LANES)
        out_copy(c).start()

    plain[8].wait()
    for x in range(2):
        ground = out[pl.ds(x, species, stride=ROWS), :]
        grad[pl.ds(x, emis.shape[0], stride=2), :] = jnp.dot(
            emis[...], ground, precision=lax.Precision.HIGHEST, preferred_element_type=F32
        )
    grad_copy = pltpu.make_async_copy(grad, grad_h, out_sem.at[nblocks])
    grad_copy.start()

    @pl.loop(0, nblocks)
    def _(c):
        @pl.when(me < n - 1)
        def _():
            block_right(c).wait_send()

        @pl.when(me > 0)
        def _():
            block_left(c).wait_send()

        out_copy(c).wait()

    @pl.when(me < n - 1)
    def _():
        to_right(small, small_l, ssem.at[0], ssem.at[1]).wait_send()

    @pl.when(me > 0)
    def _():
        to_left(small, small_r, ssem.at[2], ssem.at[3]).wait_send()

    @pl.loop(1, n)
    def _(k):
        stat_copy(k).wait_send()

    grad_copy.wait()


def body(
    lam_in, conc, jac_diag, jac_off, block_rows, block_cols, active, courant, kz, airmass, target, emis_map
):
    species, levels, width, ny = lam_in.shape
    n = lax.axis_size("col")
    nblocks, bsize = jac_diag.shape[:2]
    slots = jac_off.shape[0]
    cells = levels * width * ny * n
    fields = emis_map.shape[0]

    def flat(x):
        return x.reshape(-1, ny)

    operands = [
        flat(lam_in), flat(conc), flat(jac_diag), flat(jac_off), flat(block_rows), flat(block_cols),
        flat(active), flat(courant), kz, flat(airmass), target.reshape(1, species), emis_map,
    ]
    big = (species * ROWS, ny)
    held = [pltpu.VMEM(x.shape, x.dtype) for x in operands]
    dma = pltpu.SemaphoreType.DMA
    out, grad = pl.pallas_call(
        functools.partial(kernel, nblocks, bsize, slots, levels, cells, n),
        out_shape=(
            jax.ShapeDtypeStruct(big, F32),
            jax.ShapeDtypeStruct((fields * width, ny), F32),
        ),
        in_specs=[pl.BlockSpec(memory_space=pl.ANY)] * len(operands),
        out_specs=(pl.BlockSpec(memory_space=pl.ANY),) * 2,
        scratch_shapes=held
        + [
            pltpu.VMEM(big, F32), pltpu.VMEM(big, F32), pltpu.VMEM(big, F32), pltpu.VMEM(big, F32),
            pltpu.VMEM((fields * width, ny), F32),
            pltpu.VMEM((slots, bsize, ROWS, ny), F32),
            pltpu.VMEM((levels, ROWS, ny), F32),
            pltpu.VMEM((24, ny), F32), pltpu.VMEM((24, ny), F32), pltpu.VMEM((24, ny), F32),
            pltpu.VMEM((2, species, ny), F32),
            pltpu.VMEM((4, ny), F32), pltpu.VMEM((n, 4, ny), F32),
            pltpu.VMEM((species, ny), F32), pltpu.VMEM((species, ny), F32),
            dma((10,)), dma((slots,)), dma((nblocks,)), dma((nblocks + 1,)),
            dma((nblocks,)), dma((nblocks,)), dma((nblocks,)), dma((nblocks,)),
            dma((4,)), dma((n,)), dma((n,)),
        ],
        compiler_params=pltpu.CompilerParams(
            collective_id=0, has_side_effects=True, vmem_limit_bytes=60 * 2**20
        ),
        cost_estimate=pl.CostEstimate(flops=8_000_000, bytes_accessed=10_000_000, transcendentals=0),
    )(*operands)
    return out.reshape(lam_in.shape), grad.reshape(fields, width, ny)


def solution(mesh):
    return jax.shard_map(
        body,
        mesh=mesh,
        in_specs=(
            P("grp", None, "col", None),
            P("grp", None, "col", None),
            P("grp", None, None, None, "col", None),
            P("grp", None, None, None, "col", None),
            P("grp", None, "col", None),
            P("grp", None, "col", None),
            P("grp", "col", None),
            P(None, "grp", "col", None),
            P("grp", "col", None),
            P("grp", "col", None),
            P("grp"),
            P(),
        ),
        out_specs=(P("grp", None, "col", None), P("grp", "col", None)),
        check_vma=False,
    )
```

time: 77.8 us -> 28.5 us (0.37); the launches traced: 76.4 us -> 28 us
  blocking collectives: 29 us -> 0 us
  Pallas kernels: 0 us -> 23.7 us
  other arithmetic: 18.8 us -> 0 us
  waiting for transfers between devices: 12.6 us -> 0 us
  starting transfers between devices: 11.1 us -> 0 us
    psum x1 -> x0, blocking collectives: 29 us -> none  [body(): mass, quad = lax.psum((mass_local, quad_local), 'col')]
    pallas_call x0 -> x1, Pallas kernels: none -> 23.7 us  [body(): pl.pallas_call(functools.partial(kernel, nblocks, bsize, slots, levels, c...]
    unnamed x2 -> x0, other arithmetic: 13.5 us -> none
    ppermute x4 -> x0, waiting for transfers between devices: 12.6 us -> none  [the longest x2 12.6 us: with_halo(): lax.ppermute(tail, axis, [(i, (i + 1) % count) for i in range(ends)])]
    ppermute x4 -> x0, starting transfers between devices: 11.1 us -> none  [the longest x2 7.28 us: with_halo(): lax.ppermute(head, axis, [((i + 1) % count, i) for i in range(ends)])]
    reduce_sum x2 -> x0, other arithmetic: 2.65 us -> none  [the longest x1 2.35 us: chem_adjoint(): chosen = jnp.sum(pick[:, None] * lamb, axis=0)]
    unnamed x14 -> x2, local copies, waits for them, and re-layouts: 2.07 us -> 3.62 us
    eq x2 -> x0, local copies, waits for them, and re-layouts: 1.55 us -> none  [the longest x1 0.81 us: chem_adjoint(): block_rows[slot][None] == blocks[:, None, None, None]]
  transfers between devices with their start and end apart: 4 -> 0, of which waited for: 2 -> 0; matrix products, arithmetic and copies ran while one was open for 0% -> 0% of each run, Pallas kernels for 0% -> 0%
where the time goes in v1:
time: 28.5 us; the launch traced here: 28 us
  Pallas kernels  23.7 us (83%)
  local copies, waits for them, and re-layouts  3.62 us (13%)
  between operations  0.64 us (2%)
    pallas_call x1, Pallas kernels, body(): pl.pallas_call(functools.partial(kernel, nblocks, bsize, slots, levels, c...  23.7 us
    unnamed x2, local copies, waits for them, and re-layouts  3.62 us

profile of v1, /device:TPU:4, one launch (start us, length us, event | category | flops | bytes accessed | tf_op | source)
XLA Modules:
  0.0 28.0 jit_solution(13953254640234101408)
XLA Ops:
  0.6 23.7 %shard_map.131 = (f32[1280,128]{1,0:T(8,128)}, f32[128,128]{1,0:T(8,128)}) custom-call(f32[1280,128]{1,0:T(8,128)} %bitcast.15, f32[1280,128]{1,0:T(8,128)} %bitcast.16, bf16[20480,128]{1,0:T(8,128)(2,1)} %bitcast.12, bf16[8192,128]{1,0:T(8,128)(2,1)} %bitcast.13, s32[32,128]{1,0:T(8,128)} %bitcast.18, s32[32,128]{1,0:T(8,128)} %bitcast.19, ...), custom_call_target="tpu_custom_call" | custom-call | flops 8000000 | bytes 10000000 | tf_op jit(solution)/shard_map/pallas_call | solution.py:375
  24.4 2.1 %copy.16 = f32[160,4,2,128]{3,2,1,0:T(2,128)} copy(f32[160,4,2,128]{3,2,1,0:T(2,128)} %bitcast.14) | data formatting | bytes 1310720
  26.5 1.5 %copy.17 = f32[64,2,128]{2,1,0:T(2,128)} copy(f32[64,2,128]{2,1,0:T(2,128)} %bitcast.17) | data formatting | bytes 131072

commit v2 on v1

--- a/solution.py
+++ b/solution.py
@@ -58,12 +58,12 @@
 
 def kernel(
     nblocks, bsize, slots, levels, cells, n,
-    lam_h, conc_h, jd_h, jo_h, rows_h, cols_h, act_h, cour_h, kz_h, air_h, target_h, emis_h,
-    out_h, grad_h,
-    lam, conc, jd, jo, rows, cols, act, cour, kz, air, target, emis,
-    l0, left, right, out, grad, contrib, solve, small, small_l, small_r,
+    lam_h, conc_h, jd_h, jo_h, rows_h, cols_h, act_h, cour_h, kz_h, air_h, target_h,
+    out_h,
+    lam, conc, jd, jo, rows, cols, act, cour, kz, air, target,
+    l0, left, right, contrib, solve, small, small_l, small_r,
     part, stat, stats, scol, gcol,
-    in_sem, jo_sem, jd_sem, out_sem, send_r, send_l, recv_l, recv_r, ssem, stat_send, stat_recv,
+    in_sem, jo_sem, jd_sem, send_r, send_l, recv_l, recv_r, ssem, stat_send, stat_recv,
 ):
     me = lax.axis_index("col")
     species = nblocks * bsize
@@ -86,7 +86,7 @@
         for k, (src, dst) in enumerate(
             [
                 (lam_h, lam), (rows_h, rows), (cols_h, cols), (act_h, act), (kz_h, kz),
-                (cour_h, cour), (air_h, air), (target_h, target), (emis_h, emis), (conc_h, conc),
+                (cour_h, cour), (air_h, air), (target_h, target), (conc_h, conc),
             ]
         )
     ]
@@ -106,8 +106,7 @@
     for c in range(nblocks):
         jd_copy(c).start()
         if c == 0:
-            plain[9].start()
-    plain[8].start()
+            plain[8].start()
 
     @pl.when(me == 0)
     def _():
@@ -178,6 +177,17 @@
     def block_left(c):
         return to_left(l0.at[block_at(c)], right.at[block_at(c)], send_l.at[c], recv_r.at[c])
 
+    early = nblocks // 2
+
+    def send_block(c):
+        @pl.when(me < n - 1)
+        def _():
+            block_right(c).start()
+
+        @pl.when(me > 0)
+        def _():
+            block_left(c).start()
+
     small_right = to_right(small, small_l, ssem.at[0], ssem.at[1])
     small_left = to_left(small, small_r, ssem.at[2], ssem.at[3])
 
@@ -189,7 +199,7 @@
     def _():
         small_left.start()
 
-    plain[9].wait()
+    plain[8].wait()
 
     @pl.loop(0, nblocks)
     def _(c):
@@ -204,13 +214,9 @@
             acc = acc + jnp.where(place[None], contrib[p], 0.0)
         l0[block_at(c), :] = solve_levels(acc).reshape(bl, LANES)
 
-        @pl.when(me < n - 1)
-        def _():
-            block_right(c).start()
-
-        @pl.when(me > 0)
-        def _():
-            block_left(c).start()
+        @pl.when(c < early)
+        def _():
+            send_block(c)
 
         amount = conc[block_at(c), :].reshape(bsize, ROWS, LANES)
         at = pl.ds(pl.multiple_of(c * bsize, bsize), bsize)
@@ -242,6 +248,10 @@
     @pl.loop(1, n)
     def _(k):
         stat_copy(k).start()
+
+    @pl.loop(early, nblocks)
+    def _(c):
+        send_block(c)
 
     @pl.when(me > 0)
     def _():
@@ -295,9 +305,6 @@
         scol[first : first + LANES, :] = jnp.broadcast_to(scale, (LANES, LANES)).T
         gcol[first : first + LANES, :] = jnp.broadcast_to(gain, (LANES, LANES)).T
 
-    def out_copy(c):
-        return pltpu.make_async_copy(out.at[block_at(c)], out_h.at[block_at(c)], out_sem.at[c])
-
     @pl.loop(0, nblocks)
     def _(c):
         @pl.when(me > 0)
@@ -313,17 +320,7 @@
         moved = advect(l0[at, :].reshape(shape), left[at, :].reshape(shape), right[at, :].reshape(shape))
         names = pl.ds(pl.multiple_of(c * bsize, bsize), bsize)
         result = scol[names, :][:, None, :] * moved - gcol[names, :][:, None, :] * air_out[None]
-        out[at, :] = result.reshape(bl, LANES)
-        out_copy(c).start()
-
-    plain[8].wait()
-    for x in range(2):
-        ground = out[pl.ds(x, species, stride=ROWS), :]
-        grad[pl.ds(x, emis.shape[0], stride=2), :] = jnp.dot(
-            emis[...], ground, precision=lax.Precision.HIGHEST, preferred_element_type=F32
-        )
-    grad_copy = pltpu.make_async_copy(grad, grad_h, out_sem.at[nblocks])
-    grad_copy.start()
+        out_h[at, :] = result.reshape(bl, LANES)
 
     @pl.loop(0, nblocks)
     def _(c):
@@ -335,8 +332,6 @@
         def _():
             block_left(c).wait_send()
 
-        out_copy(c).wait()
-
     @pl.when(me < n - 1)
     def _():
         to_right(small, small_l, ssem.at[0], ssem.at[1]).wait_send()
@@ -349,6 +344,19 @@
     def _(k):
         stat_copy(k).wait_send()
 
+
+def finish(nblocks, value, emis, out_h, grad_h, grad, sem):
+    species, fields = emis.shape[1], emis.shape[0]
+    lam_copy = pltpu.make_async_copy(value, out_h, sem.at[0])
+    lam_copy.start()
+    for x in range(2):
+        ground = value[pl.ds(x, species, stride=ROWS), :]
+        grad[pl.ds(x, fields, stride=2), :] = jnp.dot(
+            emis[...], ground, precision=lax.Precision.HIGHEST, preferred_element_type=F32
+        )
+    grad_copy = pltpu.make_async_copy(grad, grad_h, sem.at[1])
+    grad_copy.start()
+    lam_copy.wait()
     grad_copy.wait()
 
 
@@ -367,30 +375,27 @@
 
     operands = [
         flat(lam_in), flat(conc), flat(jac_diag), flat(jac_off), flat(block_rows), flat(block_cols),
-        flat(active), flat(courant), kz, flat(airmass), target.reshape(1, species), emis_map,
+        flat(active), flat(courant), kz, flat(airmass), target.reshape(1, species),
     ]
     big = (species * ROWS, ny)
     held = [pltpu.VMEM(x.shape, x.dtype) for x in operands]
     dma = pltpu.SemaphoreType.DMA
-    out, grad = pl.pallas_call(
+    whole = pl.BlockSpec(memory_space=pltpu.VMEM)
+    value = pl.pallas_call(
         functools.partial(kernel, nblocks, bsize, slots, levels, cells, n),
-        out_shape=(
-            jax.ShapeDtypeStruct(big, F32),
-            jax.ShapeDtypeStruct((fields * width, ny), F32),
-        ),
-        in_specs=[pl.BlockSpec(memory_space=pl.ANY)] * len(operands),
-        out_specs=(pl.BlockSpec(memory_space=pl.ANY),) * 2,
+        out_shape=pltpu.VMEM(big, F32),
+        in_specs=[pl.BlockSpec(memory_space=pltpu.HBM)] * len(operands),
+        out_specs=whole,
         scratch_shapes=held
         + [
-            pltpu.VMEM(big, F32), pltpu.VMEM(big, F32), pltpu.VMEM(big, F32), pltpu.VMEM(big, F32),
-            pltpu.VMEM((fields * width, ny), F32),
+            pltpu.VMEM(big, F32), pltpu.VMEM(big, F32), pltpu.VMEM(big, F32),
             pltpu.VMEM((slots, bsize, ROWS, ny), F32),
             pltpu.VMEM((levels, ROWS, ny), F32),
             pltpu.VMEM((24, ny), F32), pltpu.VMEM((24, ny), F32), pltpu.VMEM((24, ny), F32),
             pltpu.VMEM((2, species, ny), F32),
             pltpu.VMEM((4, ny), F32), pltpu.VMEM((n, 4, ny), F32),
             pltpu.VMEM((species, ny), F32), pltpu.VMEM((species, ny), F32),
-            dma((10,)), dma((slots,)), dma((nblocks,)), dma((nblocks + 1,)),
+            dma((9,)), dma((slots,)), dma((nblocks,)),
             dma((nblocks,)), dma((nblocks,)), dma((nblocks,)), dma((nblocks,)),
             dma((4,)), dma((n,)), dma((n,)),
         ],
@@ -399,6 +404,19 @@
         ),
         cost_estimate=pl.CostEstimate(flops=8_000_000, bytes_accessed=10_000_000, transcendentals=0),
     )(*operands)
+    hbm = pl.BlockSpec(memory_space=pltpu.HBM)
+    out, grad = pl.pallas_call(
+        functools.partial(finish, nblocks),
+        out_shape=(
+            jax.ShapeDtypeStruct(big, F32),
+            jax.ShapeDtypeStruct((fields * width, ny), F32),
+        ),
+        in_specs=[whole, whole],
+        out_specs=(hbm, hbm),
+        scratch_shapes=[pltpu.VMEM((fields * width, ny), F32), dma((2,))],
+        compiler_params=pltpu.CompilerParams(vmem_limit_bytes=4 * 2**20),
+        cost_estimate=pl.CostEstimate(flops=6_000_000, bytes_accessed=1_400_000, transcendentals=0),
+    )(value, emis_map)
     return out.reshape(lam_in.shape), grad.reshape(fields, width, ny)
 
 

time: 28.5 us -> 23.7 us (0.83); the launches traced: 28 us -> 23.5 us
  local copies, waits for them, and re-layouts: 3.62 us -> 0.01 us
  Pallas kernels: 23.7 us -> 22.9 us
    unnamed x2, local copies, waits for them, and re-layouts: 3.62 us -> 0.01 us
    pallas_call x1, Pallas kernels: 23.7 us -> 21.9 us  [body(): pl.pallas_call(functools.partial(kernel, nblocks, bsize, slots, levels, c...]
    pallas_call x0 -> x1, Pallas kernels: none -> 0.95 us  [body(): pl.pallas_call(functools.partial(finish, nblocks), out_shape=(jax.ShapeDt...]
where the time goes in v2:
time: 23.7 us; the launch traced here: 23.5 us
  Pallas kernels  22.9 us (97%)
  between operations  0.66 us (3%)
    pallas_call x1, Pallas kernels, body(): pl.pallas_call(functools.partial(kernel, nblocks, bsize, slots, levels, c...  21.9 us
    pallas_call x1, Pallas kernels, body(): pl.pallas_call(functools.partial(finish, nblocks), out_shape=(jax.ShapeDt...  0.95 us

profile of v2, /device:TPU:4, one launch (start us, length us, event | category | flops | bytes accessed | tf_op | source)
XLA Modules:
  0.0 23.5 jit_solution(4385969805457962330)
XLA Ops:
  0.6 0.0 copy-start
  0.6 21.9 %shard_map.131.value = f32[1280,128]{1,0:T(8,128)S(1)} custom-call(f32[1280,128]{1,0:T(8,128)} %bitcast.14, f32[1280,128]{1,0:T(8,128)} %bitcast.15, bf16[20480,128]{1,0:T(8,128)(2,1)} %bitcast.12, bf16[8192,128]{1,0:T(8,128)(2,1)} %bitcast.13, s32[32,128]{1,0:T(8,128)} %bitcast.16, s32[32,128]{1,0:T(8,128)} %bitcast.17, s32[8,128]{1,0:T(8,128)} %bitcast.19, ...), custom_call_target="tpu_custom_call" | custom-call | flops 8000000 | bytes 10000000 | tf_op jit(solution)/shard_map/pallas_call | solution.py:384
  22.6 0.0 copy-done
  22.6 0.9 %shard_map.132 = (f32[1280,128]{1,0:T(8,128)}, f32[128,128]{1,0:T(8,128)}) custom-call(f32[1280,128]{1,0:T(8,128)S(1)} %shard_map.131.value, f32[64,160]{1,0:T(8,128)S(1)} %copy-done), custom_call_target="tpu_custom_call" | custom-call | flops 6000000 | bytes 1400000 | tf_op jit(solution)/shard_map/pallas_call | solution.py:408
Async XLA Ops:
  0.6 21.9 %copy-start = (f32[64,160]{1,0:T(8,128)S(1)}, f32[64,160]{1,0:T(8,128)}, u32[]{:S(2)}) copy-start(f32[64,160]{1,0:T(8,128)} %emis.1) | copy-start | bytes 122884

commit v3 on v2

--- a/solution.py
+++ b/solution.py
@@ -63,7 +63,7 @@
     lam, conc, jd, jo, rows, cols, act, cour, kz, air, target,
     l0, left, right, contrib, solve, small, small_l, small_r,
     part, stat, stats, scol, gcol,
-    in_sem, jo_sem, jd_sem, send_r, send_l, recv_l, recv_r, ssem, stat_send, stat_recv,
+    relayed, in_sem, jo_sem, jd_sem, send_r, send_l, recv_l, recv_r, relay_send, relay_recv, ssem, stat_send, stat_recv,
 ):
     me = lax.axis_index("col")
     species = nblocks * bsize
@@ -179,12 +179,66 @@
 
     early = nblocks // 2
 
+    relaying = n == 16
+    place4, plane = lax.rem(me, 4), me // 4
+    relay_until = nblocks - 4
+    from_left_flow = (place4 == 0) & (plane > 0)
+    from_right_flow = (place4 == 3) & (plane < 3)
+    relay_left = (place4 == 2) & (plane > 0)
+    relay_right = (place4 == 1) & (plane < 3)
+    share = jnp.where(place4 % 2 == 0, 2 * plane, 6 - 2 * plane)
+
+    def takes_relay(c):
+        return (c < relay_until) & (lax.rem(c * share, relay_until) < share)
+
+    def to_relay(c, offset, sems):
+        return pltpu.make_async_remote_copy(
+            src_ref=l0.at[block_at(c)], dst_ref=relayed.at[block_at(c)],
+            send_sem=sems.at[c], recv_sem=relay_recv.at[c],
+            device_id={"col": lax.rem(me + n + offset, n)}, device_id_type=pl.DeviceIdType.MESH,
+        )
+
+    def onward(c, offset, dst, sems):
+        return pltpu.make_async_remote_copy(
+            src_ref=relayed.at[block_at(c)], dst_ref=dst.at[block_at(c)],
+            send_sem=relay_send.at[c], recv_sem=sems.at[c],
+            device_id={"col": lax.rem(me + n + offset, n)}, device_id_type=pl.DeviceIdType.MESH,
+        )
+
+    def forward(c):
+        @pl.when(relay_left & takes_relay(c))
+        def _():
+            to_relay(c, 2, send_l).wait_recv()
+            onward(c, -3, right, recv_r).start()
+
+        @pl.when(relay_right & takes_relay(c))
+        def _():
+            to_relay(c, -2, send_r).wait_recv()
+            onward(c, 3, left, recv_l).start()
+
     def send_block(c):
-        @pl.when(me < n - 1)
+        if relaying:
+            detour_right = from_right_flow & takes_relay(c)
+            detour_left = from_left_flow & takes_relay(c)
+
+            @pl.when(detour_right)
+            def _():
+                to_relay(c, -2, send_r).start()
+
+            @pl.when(detour_left)
+            def _():
+                to_relay(c, 2, send_l).start()
+
+            direct_right = (me < n - 1) & jnp.logical_not(detour_right)
+            direct_left = (me > 0) & jnp.logical_not(detour_left)
+        else:
+            direct_right, direct_left = me < n - 1, me > 0
+
+        @pl.when(direct_right)
         def _():
             block_right(c).start()
 
-        @pl.when(me > 0)
+        @pl.when(direct_left)
         def _():
             block_left(c).start()
 
@@ -253,6 +307,12 @@
     def _(c):
         send_block(c)
 
+    if relaying:
+
+        @pl.loop(0, early)
+        def _(c):
+            forward(c)
+
     @pl.when(me > 0)
     def _():
         to_right(small, small_l, ssem.at[0], ssem.at[1]).wait_recv()
@@ -307,6 +367,12 @@
 
     @pl.loop(0, nblocks)
     def _(c):
+        if relaying:
+
+            @pl.when(c < relay_until - early)
+            def _():
+                forward(c + early)
+
         @pl.when(me > 0)
         def _():
             block_right(c).wait_recv()
@@ -331,6 +397,12 @@
         @pl.when(me > 0)
         def _():
             block_left(c).wait_send()
+
+        if relaying:
+
+            @pl.when((relay_left | relay_right) & takes_relay(c))
+            def _():
+                onward(c, 3, left, recv_l).wait_send()
 
     @pl.when(me < n - 1)
     def _():
@@ -395,9 +467,10 @@
             pltpu.VMEM((2, species, ny), F32),
             pltpu.VMEM((4, ny), F32), pltpu.VMEM((n, 4, ny), F32),
             pltpu.VMEM((species, ny), F32), pltpu.VMEM((species, ny), F32),
+            pltpu.VMEM(big, F32),
             dma((9,)), dma((slots,)), dma((nblocks,)),
             dma((nblocks,)), dma((nblocks,)), dma((nblocks,)), dma((nblocks,)),
-            dma((4,)), dma((n,)), dma((n,)),
+            dma((nblocks,)), dma((nblocks,)), dma((4,)), dma((n,)), dma((n,)),
         ],
         compiler_params=pltpu.CompilerParams(
             collective_id=0, has_side_effects=True, vmem_limit_bytes=60 * 2**20

time: 23.7 us -> 22.6 us (0.954)
  Pallas kernels: 22.9 us -> 21.8 us
    pallas_call x1, Pallas kernels: 21.9 us -> 20.8 us  [body(): pl.pallas_call(functools.partial(kernel, nblocks, bsize, slots, levels, c...]
where the time goes in v3:
time: 22.6 us; the launch traced here: 22.4 us
  Pallas kernels  21.8 us (96%)
  between operations  0.66 us (3%)
    pallas_call x1, Pallas kernels, body(): pl.pallas_call(functools.partial(kernel, nblocks, bsize, slots, levels, c...  20.8 us
    pallas_call x1, Pallas kernels, body(): pl.pallas_call(functools.partial(finish, nblocks), out_shape=(jax.ShapeDt...  0.95 us

profile of v3, /device:TPU:4, one launch (start us, length us, event | category | flops | bytes accessed | tf_op | source)
XLA Modules:
  0.0 22.4 jit_solution(16679942518610394765)
XLA Ops:
  0.6 0.0 copy-start
  0.6 20.8 %shard_map.131.value = f32[1280,128]{1,0:T(8,128)S(1)} custom-call(f32[1280,128]{1,0:T(8,128)} %bitcast.14, f32[1280,128]{1,0:T(8,128)} %bitcast.15, bf16[20480,128]{1,0:T(8,128)(2,1)} %bitcast.12, bf16[8192,128]{1,0:T(8,128)(2,1)} %bitcast.13, s32[32,128]{1,0:T(8,128)} %bitcast.16, s32[32,128]{1,0:T(8,128)} %bitcast.17, s32[8,128]{1,0:T(8,128)} %bitcast.19, ...), custom_call_target="tpu_custom_call" | custom-call | flops 8000000 | bytes 10000000 | tf_op jit(solution)/shard_map/pallas_call | solution.py:456
  21.5 0.0 copy-done
  21.5 0.9 %shard_map.132 = (f32[1280,128]{1,0:T(8,128)}, f32[128,128]{1,0:T(8,128)}) custom-call(f32[1280,128]{1,0:T(8,128)S(1)} %shard_map.131.value, f32[64,160]{1,0:T(8,128)S(1)} %copy-done), custom_call_target="tpu_custom_call" | custom-call | flops 6000000 | bytes 1400000 | tf_op jit(solution)/shard_map/pallas_call | solution.py:481
Async XLA Ops:
  0.6 20.8 %copy-start = (f32[64,160]{1,0:T(8,128)S(1)}, f32[64,160]{1,0:T(8,128)}, u32[]{:S(2)}) copy-start(f32[64,160]{1,0:T(8,128)} %emis.1) | copy-start | bytes 122884

commit v4 on v3

--- a/solution.py
+++ b/solution.py
@@ -99,10 +99,12 @@
         at = pl.ds(pl.multiple_of(c * step, step), step)
         return pltpu.make_async_copy(jd_h.at[at], jd.at[at], jd_sem.at[c])
 
-    for copy in plain[:8]:
-        copy.start()
+    for k in (0, 1, 3):
+        plain[k].start()
     for p in range(slots):
         jo_copy(p).start()
+    for k in (2, 4, 5, 6, 7):
+        plain[k].start()
     for c in range(nblocks):
         jd_copy(c).start()
         if c == 0:
@@ -118,24 +120,8 @@
         right[...] = jnp.zeros_like(right)
         small_r[...] = jnp.zeros_like(small_r)
 
-    for copy in plain[1:8]:
-        copy.wait()
-
-    kzs = [kz[lev] for lev in range(levels - 1)]
-    inverse = inverse_levels(kzs)
-    for shift in range(levels):
-        for lev in range(levels):
-            solve[shift, 2 * lev : 2 * lev + 2, :] = inverse[lev][(lev - shift) % levels]
-
-    def solve_levels(x):
-        total = x * solve[0]
-        for shift in range(1, levels):
-            total = total + pltpu.roll(x, 2 * shift, x.ndim - 2) * solve[shift]
-        return total
-
-    small[0:8, :] = cour[0:8, :]
-    small[8:16, :] = cour[8:16, :]
-    small[16:24, :] = solve_levels(air[...])
+    for k in (1, 3):
+        plain[k].wait()
 
     plain[0].wait()
 
@@ -154,6 +140,25 @@
             acc = acc + jo[at, :].astype(F32).reshape(bsize, ROWS, LANES) * chosen[i][None]
         contrib[p] = acc
 
+    for k in (2, 4, 5, 6, 7):
+        plain[k].wait()
+
+    kzs = [kz[lev] for lev in range(levels - 1)]
+    inverse = inverse_levels(kzs)
+    for shift in range(levels):
+        for lev in range(levels):
+            solve[shift, 2 * lev : 2 * lev + 2, :] = inverse[lev][(lev - shift) % levels]
+
+    def solve_levels(x):
+        total = x * solve[0]
+        for shift in range(1, levels):
+            total = total + pltpu.roll(x, 2 * shift, x.ndim - 2) * solve[shift]
+        return total
+
+    small[0:8, :] = cour[0:8, :]
+    small[8:16, :] = cour[8:16, :]
+    small[16:24, :] = solve_levels(air[...])
+
     pl.semaphore_wait(barrier, n - 1)
 
     def to_right(src, dst, ssem_, rsem):
@@ -177,7 +182,7 @@
     def block_left(c):
         return to_left(l0.at[block_at(c)], right.at[block_at(c)], send_l.at[c], recv_r.at[c])
 
-    early = nblocks // 2
+    early = nblocks // 2 - 2
 
     relaying = n == 16
     place4, plane = lax.rem(me, 4), me // 4

time: 22.6 us -> 22.6 us (level)
  no operation moved by 1% of the time
where the time goes in v4:
time: 22.6 us; the launch traced here: 22.4 us
  Pallas kernels  21.8 us (96%)
  between operations  0.66 us (3%)
    pallas_call x1, Pallas kernels, body(): pl.pallas_call(functools.partial(kernel, nblocks, bsize, slots, levels, c...  20.8 us
    pallas_call x1, Pallas kernels, body(): pl.pallas_call(functools.partial(finish, nblocks), out_shape=(jax.ShapeDt...  0.95 us

profile of v4, /device:TPU:4, one launch (start us, length us, event | category | flops | bytes accessed | tf_op | source)
XLA Modules:
  0.0 22.4 jit_solution(5641455765640668738)
XLA Ops:
  0.6 0.0 copy-start
  0.6 20.8 %shard_map.131.value = f32[1280,128]{1,0:T(8,128)S(1)} custom-call(f32[1280,128]{1,0:T(8,128)} %bitcast.14, f32[1280,128]{1,0:T(8,128)} %bitcast.15, bf16[20480,128]{1,0:T(8,128)(2,1)} %bitcast.12, bf16[8192,128]{1,0:T(8,128)(2,1)} %bitcast.13, s32[32,128]{1,0:T(8,128)} %bitcast.16, s32[32,128]{1,0:T(8,128)} %bitcast.17, s32[8,128]{1,0:T(8,128)} %bitcast.19, ...), custom_call_target="tpu_custom_call" | custom-call | flops 8000000 | bytes 10000000 | tf_op jit(solution)/shard_map/pallas_call | solution.py:461
  21.5 0.0 copy-done
  21.5 0.9 %shard_map.132 = (f32[1280,128]{1,0:T(8,128)}, f32[128,128]{1,0:T(8,128)}) custom-call(f32[1280,128]{1,0:T(8,128)S(1)} %shard_map.131.value, f32[64,160]{1,0:T(8,128)S(1)} %copy-done), custom_call_target="tpu_custom_call" | custom-call | flops 6000000 | bytes 1400000 | tf_op jit(solution)/shard_map/pallas_call | solution.py:486
Async XLA Ops:
  0.6 20.8 %copy-start = (f32[64,160]{1,0:T(8,128)S(1)}, f32[64,160]{1,0:T(8,128)}, u32[]{:S(2)}) copy-start(f32[64,160]{1,0:T(8,128)} %emis.1) | copy-start | bytes 122884
